TPU v7x, 32 devices: a whole 2x2x4 slice. The times are simulated.
32 devices in a mesh: tp: 2 (over core), row: 4 (over y, x), col: 4 (over z).
Axes of the slice: x: 2, y: 2, z: 4, core: 2. Of those that a mesh axis runs over, the one named last changes fastest.
Arguments:
- acts: bfloat16 [128, 128, 4096], P(('row', 'col'), None, 'tp'), may hold values from -6 to 6
- grads: bfloat16 [128, 128, 4096], P(('row', 'col'), None, 'tp'), may hold values from -6 to 6
- proj_in: bfloat16 [4096, 192], P('tp'), may hold values from -0.09375 to 0.09375
- proj_out: bfloat16 [4096, 64], P('tp'), may hold values from -0.09375 to 0.09375
- curvature: float32 [12288, 12288], P('row', ('tp', 'col')), may hold values from -1 to 7, as said below
Outputs:
- trailing: float32 [12288, 12288], P('row', ('tp', 'col'))
- panel: float32 [12288, 512], P('row', 'tp')
Inputs may be any that keep to these rules, and one draw needn't show every extreme that they name: curvature is symmetric.
All inputs are finite; a program needn't handle non-finite values.
Results may differ from a plain program's by a relative error of at most 0.0021.
Values may be sent and summed in bfloat16 or wider, within the bound.
A program may use at most 128 MiB of HBM per device.

v0:
```python
import jax
import jax.numpy as jnp
from jax import lax
from jax.sharding import PartitionSpec as P

PANEL = 512


precise = lax.Precision.HIGHEST


def spread(block, axis, source):
    block = jnp.where(lax.axis_index(axis) == source, block, jnp.zeros_like(block))
    return lax.psum(block, axis)


def per_device(acts, grads, proj_in, proj_out, curvature):
    tp_count = lax.axis_size("tp")
    row_count = lax.axis_size("row")
    col_count = lax.axis_size("col")
    tp_index = lax.axis_index("tp")
    col_index = lax.axis_index("col")
    ex_dev, seq_len, width = acts.shape
    rows_blk, cols_blk = curvature.shape
    act_width = proj_in.shape[1]
    grad_width = proj_out.shape[1]
    examples = ex_dev * row_count * col_count
    scale = (seq_len * examples) ** (-0.5)
    act_part = jnp.dot(
        acts.reshape(-1, width), proj_in, preferred_element_type=jnp.float32
    ).reshape(ex_dev, seq_len, act_width)
    grad_part = jnp.dot(
        grads.reshape(-1, width), proj_out, preferred_element_type=jnp.float32
    ).reshape(ex_dev, seq_len, grad_width)
    proj_acts, proj_grads = lax.psum((act_part, grad_part), "tp")
    col_width = act_width // (tp_count * col_count)
    act_cols = lax.dynamic_index_in_dim(
        proj_acts.reshape(ex_dev, seq_len, tp_count, col_count, col_width),
        tp_index,
        2,
        keepdims=False,
    )
    col_local = (
        jnp.einsum("escw,esj->cewj", act_cols, proj_grads, precision=precise) * scale
    ).astype(jnp.bfloat16)
    col_local = col_local.reshape(col_count, ex_dev, cols_blk)
    col_mine = lax.all_to_all(col_local, "col", split_axis=0, concat_axis=0, tiled=True)
    row_width = act_width // row_count
    quarter = row_width // tp_count
    act_quart = lax.dynamic_index_in_dim(
        proj_acts.reshape(ex_dev, seq_len, row_count, tp_count, quarter),
        tp_index,
        3,
        keepdims=False,
    )
    quart_local = (
        jnp.einsum("esrq,esj->reqj", act_quart, proj_grads, precision=precise) * scale
    ).astype(jnp.bfloat16)
    quart_local = quart_local.reshape(row_count, ex_dev, quarter * grad_width)
    quart_mine = lax.all_to_all(quart_local, "row", split_axis=0, concat_axis=0, tiled=True)
    quart_all = lax.all_gather(quart_mine[None], ("tp", "col"), axis=0, tiled=True)
    quart_all = quart_all.reshape(tp_count, col_count, row_count, ex_dev, quarter * grad_width)
    folded = lax.dot_general(
        quart_all,
        lax.all_gather(col_mine[:, None], "row", axis=1, tiled=True),
        (((1, 2, 3), (0, 1, 2)), ((), ())),
        preferred_element_type=jnp.float32,
    )
    updated = curvature + folded.reshape(rows_blk, cols_blk)
    panel_w = PANEL
    block_index = tp_index * col_count + col_index
    owners = -(-panel_w // cols_blk)
    contrib = jnp.where(block_index < owners, updated, jnp.zeros_like(updated))
    panel_cols = lax.psum(contrib[:, :panel_w], ("tp", "col"))
    top_block, diag_block = (
        spread(updated[:panel_w], "row", 0),
        spread(panel_cols[:panel_w], "row", 0),
    )
    diag_factor = jnp.linalg.cholesky(diag_block)
    panel_rows = jax.scipy.linalg.solve_triangular(diag_factor, panel_cols.T, lower=True).T
    top_factor = jax.scipy.linalg.solve_triangular(diag_factor, top_block, lower=True)
    trailing = updated - jnp.dot(
        panel_rows, top_factor, precision=precise, preferred_element_type=jnp.float32
    )
    width_out = panel_w // tp_count
    panel = lax.dynamic_slice_in_dim(panel_rows, tp_index * width_out, width_out, 1)
    return (trailing, panel)


def solution(mesh):
    in_specs = (
        P(("row", "col"), None, "tp"),
        P(("row", "col"), None, "tp"),
        P("tp", None),
        P("tp", None),
        P("row", ("tp", "col")),
    )
    out_specs = (P("row", ("tp", "col")), P("row", "tp"))
    return jax.shard_map(
        per_device, mesh=mesh, in_specs=in_specs, out_specs=out_specs, check_vma=False
    )
```

profile of v0, /device:TPU:0, one launch (start us, length us, event | category | flops | bytes accessed | tf_op | source)
XLA Modules:
  0.0 591.3 jit_solution(11037071170355715507)
XLA Ops:
  7.2 4.5 fusion.37
  11.7 2.5 fusion.32
  14.2 18.7 %copy.28 = f32[3072,1536]{0,1:T(8,128)} copy(f32[3072,1536]{1,0:T(8,128)} %param.9) | data formatting | bytes 37748736 | tf_op args[4]
  32.9 3.8 all-reduce.11.cloned.1.call-done
  42.7 3.9 all-to-all-start
  47.4 4.1 all-to-all-done
  51.5 4.6 all-to-all-start.1
  56.1 27.6 %all-gather = bf16[32,8,1536]{2,1,0:T(8,128)(2,1)S(1)} all-gather(bf16[4,8,1536]{2,1,0:T(8,128)(2,1)S(1)} %all-to-all-done), channel_id=2, replica_groups=mesh['tp'=2,'row'=4,'col'=4] {'tp','col'}, dimensions={0}, use_global_device_ids=true | all-gather | bytes 884736 | tf_op jit(solution)/shard_map/all_gather | solution.py:61
  83.9 9.8 %all-gather.1 = bf16[4,32,1536]{2,0,1:T(4,128)(2,1)S(1)} all-gather(bf16[4,8,1536]{2,0,1:T(4,128)(2,1)S(1)} %copy.26), channel_id=3, replica_groups=mesh['tp'=2,'row'=4,'col'=4] {'row'}, dimensions={1}, use_global_device_ids=true | all-gather | bytes 491520 | tf_op jit(solution)/shard_map/all_gather | solution.py:65
  93.7 12.1 %bitcast_add_fusion = f32[3072,1536]{0,1:T(8,128)} fusion(f32[3072,1536]{0,1:T(8,128)} %copy.28, bf16[3072,4,4,8]{0,3,2,1:T(8,128)(2,1)S(1)} %bitcast.109, bf16[4,32,1536]{2,0,1:T(4,128)(2,1)S(1)} %all-gather.1), kind=kOutput, calls=%fused_computation.2 | convolution fusion | flops 1212678144 | bytes 38928384 | tf_op jit(solution)/shard_map/dot_general | solution.py:63
  105.8 6.2 %slice_select_fusion = f32[3072,512]{0,1:T(8,128)} fusion(f32[3072,1536]{0,1:T(8,128)} %bitcast_add_fusion, pred[]{:T(512)S(6)} %lt.13), kind=kLoop, calls=%fused_computation.4 | loop fusion | flops 1572864 | bytes 12582913 | tf_op jit(solution)/shard_map/jit(_where)/select_n | solution.py:73
  112.3 3.9 slice_select_fusion.1
  116.3 130.6 %all-reduce.7.cloned.1.call-done = f32[3072,512]{0,1:T(8,128)} async-done(((f32[3072,512]{0,1:T(8,128)}), f32[3072,512]{0,1:T(8,128)}) %all-reduce.7.cloned.1.call-update) | async-done | bytes 6291472 | tf_op jit(solution)/shard_map/psum | solution.py:74
  249.2 106.5 %all-reduce.9.cloned.1.call-done = (f32[512,1536]{0,1:T(8,128)}, f32[512,512]{0,1:T(8,128)}) async-done(((f32[512,1536]{0,1:T(8,128)}, f32[512,512]{0,1:T(8,128)}), (f32[512,1536]{0,1:T(8,128)}, f32[512,512]{0,1:T(8,128)})) %all-reduce.9.cloned.1.call-update) | async-done | bytes 4194320 | tf_op jit(solution)/shard_map/psum | solution.py:14
  358.7 11.7 %cholesky.103 = f32[128,128]{1,0:T(8,128)S(1)} custom-call(f32[128,128]{1,0:T(8,128)S(1)} %cholesky.263), custom_call_target="Cholesky" | custom-call | tf_op jit(solution)/shard_map/jit(cholesky)/cholesky | solution.py:79
  370.6 9.8 %custom-call.34 = f32[1,128,128]{1,2,0:T(8,128)S(1)} custom-call(f32[1,128,128]{2,1,0:T(8,128)S(1)} %get-tuple-element.41), custom_call_target="InvertDiagBlocksLowerTriangular" | custom-call | tf_op jit(solution)/shard_map/jit(cholesky)/cholesky | solution.py:79
  381.2 11.7 %cholesky.215 = f32[128,128]{1,0:T(8,128)S(1)} custom-call(f32[128,128]{1,0:T(8,128)S(1)} %cholesky.267), custom_call_target="Cholesky" | custom-call | tf_op jit(solution)/shard_map/jit(cholesky)/cholesky | solution.py:79
  393.0 10.2 %custom-call.35 = f32[1,128,128]{1,2,0:T(8,128)S(1)} custom-call(f32[1,128,128]{2,1,0:T(8,128)S(1)} %get-tuple-element.39), custom_call_target="InvertDiagBlocksLowerTriangular" | custom-call | tf_op jit(solution)/shard_map/jit(cholesky)/cholesky | solution.py:79
  404.3 11.7 %cholesky.236 = f32[128,128]{1,0:T(8,128)S(1)} custom-call(f32[128,128]{1,0:T(8,128)S(1)} %cholesky.272), custom_call_target="Cholesky" | custom-call | tf_op jit(solution)/shard_map/jit(cholesky)/cholesky | solution.py:79
  416.2 9.8 %custom-call.36 = f32[1,128,128]{1,2,0:T(8,128)S(1)} custom-call(f32[1,128,128]{2,1,0:T(8,128)S(1)} %get-tuple-element.37), custom_call_target="InvertDiagBlocksLowerTriangular" | custom-call | tf_op jit(solution)/shard_map/jit(cholesky)/cholesky | solution.py:79
  426.8 11.9 %cholesky.253 = f32[128,128]{1,0:T(8,128)S(1)} custom-call(f32[128,128]{1,0:T(8,128)S(1)} %convolution_subtract_fusion.8), custom_call_target="Cholesky" | custom-call | tf_op jit(solution)/shard_map/jit(cholesky)/cholesky | solution.py:79
  443.6 8.8 %while.1 = (s32[]{:T(128)}, f32[512,512]{0,1:T(8,128)S(1)}, s32[4,2]{0,1:T(2,128)S(1)}, f32[4,128,128]{2,1,0:T(8,128)S(1)}, s32[]{:T(128)}) while((s32[]{:T(128)}, f32[512,512]{0,1:T(8,128)S(1)}, s32[4,2]{0,1:T(2,128)S(1)}, f32[4,128,128]{2,1,0:T(8,128)S(1)}, s32[]{:T(128)}) %tuple.31), condition=%wide.while_cond, body=%wide.while_body.sunk | while | flops 2 | bytes 393329 | solution.py:80
  452.4 39.3 %custom-call.37 = f32[4,128,128]{1,2,0:T(8,128)S(1)} custom-call(f32[4,128,128]{2,1,0:T(8,128)S(1)} %get-tuple-element.9), custom_call_target="InvertDiagBlocksLowerTriangular" | custom-call | tf_op jit(solution)/shard_map/jit(_solve_triangular)/triangular_solve | solution.py:80
  493.9 2.8 convolution_subtract_fusion.5
  497.6 3.7 convolution_subtract_fusion.3
  502.2 3.9 convolution_subtract_fusion.4
  516.0 2.9 fusion.6
  520.5 3.0 pad_maximum_fusion
  523.5 35.0 %convolution_subtract_fusion = f32[3072,1536]{0,1:T(8,128)} fusion(f32[3072,1536]{0,1:T(8,128)S(1)} %bitcast.102, f32[128,1536]{1,0:T(8,128)} %fusion.59, f32[128,1536]{1,0:T(8,128)} %copy-done.2, f32[128,1536]{1,0:T(8,128)S(1)} %fusion.55, f32[128,1536]{1,0:T(8,128)S(1)} %fusion.30, f32[128,3072]{1,0:T(8,128)S(1)} %fusion.60, f32[128,3072]{1,0:T(8,128)S(1)} %fusion.58, ...), kind=kOutput, calls=%fused_computation.3 | convolution fusion | flops 29002825728 | bytes 47185920 | tf_op jit(solution)/shard_map/dot_general | solution.py:82
  558.5 3.9 dynamic-slice_bitcast_fusion
  562.4 3.5 copy.41
  565.9 18.7 %copy.40 = f32[3072,1536]{1,0:T(8,128)} copy(f32[3072,1536]{0,1:T(8,128)} %convolution_subtract_fusion) | data formatting | bytes 37748736
  (112 shorter events, 41.8 us)
Async XLA Ops:
  7.2 4.5 copy-start
  7.2 29.5 %all-reduce.11.cloned.1.call-start = ((), (), s32[]{:S(2)}) async-start(), calls=%async_computation.4 | async-start | bytes 2097152 | tf_op jit(solution)/shard_map/psum | solution.py:35
  7.2 4.5 copy-start.6
  42.7 8.9 %all-to-all-start = ((bf16[4,8,1536]{2,1,0:T(8,128)(2,1)}), bf16[4,8,1536]{2,1,0:T(8,128)(2,1)S(1)}, u32[]{:S(2)}, u32[]{:S(2)}) async-start(bf16[4,8,1536]{2,1,0:T(8,128)(2,1)} %copy.23), calls=%async_computation | async-start | bytes 196608 | tf_op jit(solution)/shard_map/all_to_all | solution.py:60
  51.5 32.3 %all-to-all-start.1 = ((bf16[4,8,1536]{2,1,0:T(8,128)(2,1)}), bf16[4,8,1536]{2,1,0:T(8,128)(2,1)S(1)}, u32[]{:S(2)}, u32[]{:S(2)}) async-start(bf16[4,8,1536]{2,1,0:T(8,128)(2,1)} %copy.25), calls=%async_computation.1 | async-start | bytes 196608 | tf_op jit(solution)/shard_map/all_to_all | solution.py:47
  56.1 190.7 %all-reduce.7.cloned.1.call-start = ((), (), s32[]{:S(2)}) async-start(), calls=%async_computation.2 | async-start | bytes 12582912 | tf_op jit(solution)/shard_map/psum | solution.py:74
  112.1 243.6 %all-reduce.9.cloned.1.call-start = ((), (), s32[]{:S(2)}) async-start(), calls=%async_computation.3 | async-start | bytes 8388608 | tf_op jit(solution)/shard_map/psum | solution.py:14
  452.4 41.5 %copy-start.3 = (f32[512,512]{0,1:T(8,128)}, f32[512,512]{0,1:T(8,128)S(1)}, u32[]{:S(2)}) copy-start(f32[512,512]{0,1:T(8,128)S(1)} %get-tuple-element.102) | copy-start | bytes 3145732
  491.7 5.8 copy-start.5
  491.8 16.1 %slice-start.5 = ((s8[6291456]{0:T(1024)(128)(4,1)}), s8[4194304]{0:T(1024)(128)(4,1)S(1)}, s32[]{:S(2)}) async-start(s8[6291456]{0:T(1024)(128)(4,1)} %bitcast.103), calls=%async_computation.10 | async-start | bytes 8388608
  496.7 5.5 copy-start.4
  497.6 10.3 %slice-start.6 = ((s8[6291456]{0:T(1024)(128)(4,1)}), s8[2097152]{0:T(1024)(128)(4,1)S(1)}, s32[]{:S(2)}) async-start(s8[6291456]{0:T(1024)(128)(4,1)} %bitcast.103), calls=%async_computation.11 | async-start | bytes 4194304
  502.2 7.6 %copy-start.2 = (f32[128,1536]{1,0:T(8,128)}, f32[128,1536]{1,0:T(8,128)S(1)}, u32[]{:S(2)}) copy-start(f32[128,1536]{1,0:T(8,128)S(1)} %fusion.57) | copy-start | bytes 2359300
  511.3 12.2 %slice-start = ((s8[18874368]{0:T(1024)(128)(4,1)}), s8[4194304]{0:T(1024)(128)(4,1)S(1)}, s32[]{:S(2)}) async-start(s8[18874368]{0:T(1024)(128)(4,1)} %bitcast.101), calls=%async_computation.5 | async-start | bytes 8388608
  512.7 10.7 %slice-start.1 = ((s8[18874368]{0:T(1024)(128)(4,1)}), s8[4194304]{0:T(1024)(128)(4,1)S(1)}, s32[]{:S(2)}) async-start(s8[18874368]{0:T(1024)(128)(4,1)} %bitcast.101), calls=%async_computation.6 | async-start | bytes 8388608
  516.0 7.4 %slice-start.2 = ((s8[18874368]{0:T(1024)(128)(4,1)}), s8[4194304]{0:T(1024)(128)(4,1)S(1)}, s32[]{:S(2)}) async-start(s8[18874368]{0:T(1024)(128)(4,1)} %bitcast.101), calls=%async_computation.7 | async-start | bytes 8388608
  519.0 4.5 slice-start.3
  520.5 3.0 slice-start.4
  565.9 18.7 %copy-start.1 = (bf16[2048,192]{0,1:T(8,128)(2,1)S(1)}, bf16[2048,192]{0,1:T(8,128)(2,1)}, u32[]{:S(2)}) copy-start(bf16[2048,192]{0,1:T(8,128)(2,1)} %param.7) | copy-start | bytes 2359300
Sparse Core Ops, SparseCore 0:
  14.3 22.3 all-reduce.10
  112.2 134.5 all-reduce.6
  251.4 104.2 all-reduce.8
where the time goes:
time: 598 us; the launch traced here: 591 us
  waiting for transfers between devices  245 us (41%)
  other arithmetic  135 us (23%)
  matrix products  87.9 us (15%)
  local copies, waits for them, and re-layouts  59.6 us (10%)
  blocking collectives  37.4 us (6%)
  between operations  17.1 us (3%)
  starting transfers between devices  8.79 us (1%)
    psum x1, waiting for transfers between devices, per_device(): panel_cols = lax.psum(contrib[:, :panel_w], ('tp', 'col'))  131 us
    psum x1, waiting for transfers between devices, spread(): return lax.psum(block, axis)  106 us
    another operation x14, other arithmetic, per_device(): diag_factor = jnp.linalg.cholesky(diag_block)  79 us
    another operation x4, other arithmetic, per_device(): jax.scipy.linalg.solve_triangular(diag_factor, panel_cols.T, lower=True)  42.4 us
    unnamed x31, local copies, waits for them, and re-layouts  41 us
    dot_general x1, matrix products, per_device(): jnp.dot(panel_rows, top_factor, precision=precise, preferred_element_type...  35 us
    all_gather x1, blocking collectives, per_device(): lax.all_gather(quart_mine[None], ('tp', 'col'), axis=0, tiled=True)  27.6 us
    another operation x7, matrix products, per_device(): jax.scipy.linalg.solve_triangular(diag_factor, top_block, lower=True)  16 us
  transfers between devices with their start and end apart: 5, of which 4 were waited for; matrix products, arithmetic and copies ran while one was open for 4% of the time, Pallas kernels for 0%

commit v1 on v0

v1 whole, which is shorter than its diff:
```python
import functools

import jax
import jax.numpy as jnp
from jax import lax
from jax.experimental import pallas as pl
from jax.experimental.pallas import tpu as pltpu
from jax.sharding import PartitionSpec as P

PANEL = 512
NB = 128
precise = lax.Precision.HIGHEST


def factor_block(s, w):
    n = len(s)
    sub = lax.broadcasted_iota(jnp.int32, (8, NB), 0)
    s, w = list(s), list(w)
    for q in range(n):
        c = [
            [jnp.broadcast_to(s[i][:, 8 * q + j : 8 * q + j + 1], (8, NB)) for j in range(8)]
            for i in range(q, n)
        ]
        scale = jnp.zeros((8, NB), jnp.float32)
        for r in range(8):
            piv = jnp.broadcast_to(c[0][r][r : r + 1], (8, NB))
            inv = 1.0 / piv
            scale = jnp.where(sub == r, lax.rsqrt(piv), scale)
            row_s = jnp.broadcast_to(s[q][r : r + 1], (8, NB)) * inv
            row_w = jnp.broadcast_to(w[q][r : r + 1], (8, NB)) * inv
            row_c = [None] * 8
            for j in range(r + 1, 8):
                row_c[j] = jnp.broadcast_to(c[0][j][r : r + 1], (8, NB)) * inv
            for i in range(q, n):
                m = c[i - q][r]
                if i == q:
                    m = jnp.where(sub > r, m, 0.0)
                s[i] = s[i] - m * row_s
                w[i] = w[i] - m * row_w
                for j in range(r + 1, 8):
                    c[i - q][j] = c[i - q][j] - m * row_c[j]
        s[q] = s[q] * scale
        w[q] = w[q] * scale
    return s, w


def inverse_kernel(a_ref, out_ref, work):
    n = a_ref.shape[0]
    row = lax.broadcasted_iota(jnp.int32, (n, n), 0)
    col = lax.broadcasted_iota(jnp.int32, (n, n), 1)
    work[:, :n] = a_ref[...]
    work[:, n:] = jnp.where(row == col, 1.0, 0.0)
    eye = [
        jnp.where(
            lax.broadcasted_iota(jnp.int32, (8, NB), 0) + 8 * i
            == lax.broadcasted_iota(jnp.int32, (8, NB), 1),
            1.0,
            0.0,
        )
        for i in range(NB // 8)
    ]

    for b in range(n // NB):
        lo = b * NB
        s = [work[lo + 8 * i : lo + 8 * i + 8, lo : lo + NB] for i in range(NB // 8)]
        _, t = factor_block(s, eye)
        t = jnp.concatenate(t, axis=0)
        full = jnp.dot(
            t, work[lo : lo + NB, :], precision=precise, preferred_element_type=jnp.float32
        )
        work[lo : lo + NB, :] = full
        if lo + NB < n:
            left = full[:, lo + NB : n]
            work[lo + NB :, :] -= lax.dot_general(
                left,
                full,
                (((0,), (0,)), ((), ())),
                precision=precise,
                preferred_element_type=jnp.float32,
            )
    out_ref[...] = jnp.where(row >= col, work[:, n:], 0.0)


def factor_inverse(a):
    n = a.shape[0]
    return pl.pallas_call(
        inverse_kernel,
        out_shape=jax.ShapeDtypeStruct((n, n), jnp.float32),
        in_specs=[pl.BlockSpec(memory_space=pltpu.VMEM)],
        out_specs=pl.BlockSpec(memory_space=pltpu.VMEM),
        scratch_shapes=[pltpu.VMEM((n, 2 * n), jnp.float32)],
        cost_estimate=pl.CostEstimate(
            flops=40_000_000_000, bytes_accessed=8 * n * n, transcendentals=0
        ),
        compiler_params=pltpu.CompilerParams(vmem_limit_bytes=32 << 20),
    )(a)


def per_device(acts, grads, proj_in, proj_out, curvature):
    tp_count = lax.axis_size("tp")
    row_count = lax.axis_size("row")
    col_count = lax.axis_size("col")
    tp_index = lax.axis_index("tp")
    row_index = lax.axis_index("row")
    col_index = lax.axis_index("col")
    ex_dev, seq_len, width = acts.shape
    rows_blk, cols_blk = curvature.shape
    act_width = proj_in.shape[1]
    grad_width = proj_out.shape[1]
    examples = ex_dev * row_count * col_count
    scale = (seq_len * examples) ** (-0.5)
    panel_w = PANEL
    block_index = tp_index * col_count + col_index

    zero = jnp.zeros((), jnp.float32)
    first_col = block_index == 0
    first_row = row_index == 0
    diag_raw = lax.psum(
        jnp.where(first_col & first_row, curvature[:panel_w, :panel_w], zero),
        ("tp", "row", "col"),
    )
    rows_raw = lax.psum(
        jnp.where(first_col, curvature[:, :panel_w], zero), ("tp", "col")
    )
    top_raw = lax.psum(jnp.where(first_row, curvature[:panel_w], zero), "row")

    act_part = jnp.dot(
        acts.reshape(-1, width), proj_in, preferred_element_type=jnp.float32
    ).reshape(ex_dev, seq_len, act_width)
    grad_part = jnp.dot(
        grads.reshape(-1, width), proj_out, preferred_element_type=jnp.float32
    ).reshape(ex_dev, seq_len, grad_width)
    proj_acts, proj_grads = lax.psum((act_part, grad_part), "tp")
    half = act_width // tp_count
    mine = lax.dynamic_slice_in_dim(proj_acts, tp_index * half, half, 2)
    local = (
        jnp.einsum("esi,esj->eij", mine, proj_grads, precision=precise) * scale
    ).astype(jnp.bfloat16)
    local = local.reshape(ex_dev, half * grad_width)
    feats = lax.all_gather(local, ("tp", "row", "col"), axis=0)
    feats = feats.reshape(tp_count, examples, half * grad_width)

    def part(start, size):
        per = half * grad_width
        if size <= per and per % size == 0:
            one = lax.dynamic_slice(
                feats, (start // per, 0, start % per), (1, examples, size)
            )
            return one[0]
        flat = jnp.concatenate([feats[t] for t in range(tp_count)], axis=1)
        return lax.dynamic_slice_in_dim(flat, start, size, 1)

    f_rows = part(row_index * rows_blk, rows_blk)
    f_cols = part(block_index * cols_blk, cols_blk)
    f_pan = feats[0][:, :panel_w]

    def gram(a, b):
        return lax.dot_general(
            a, b, (((0,), (0,)), ((), ())), preferred_element_type=jnp.float32
        )

    inverse = factor_inverse(diag_raw + gram(f_pan, f_pan))
    rows_upd = rows_raw + gram(f_rows, f_pan)
    top_upd = top_raw + gram(f_pan, f_cols)
    panel_rows = lax.dot_general(
        rows_upd,
        inverse,
        (((1,), (1,)), ((), ())),
        precision=precise,
        preferred_element_type=jnp.float32,
    )
    top_factor = jnp.dot(
        inverse, top_upd, precision=precise, preferred_element_type=jnp.float32
    )
    trailing = (curvature + gram(f_rows, f_cols)) - jnp.dot(
        panel_rows,
        top_factor,
        precision=lax.Precision.HIGH,
        preferred_element_type=jnp.float32,
    )
    width_out = panel_w // tp_count
    panel = lax.dynamic_slice_in_dim(panel_rows, tp_index * width_out, width_out, 1)
    return (trailing, panel)


def solution(mesh):
    in_specs = (
        P(("row", "col"), None, "tp"),
        P(("row", "col"), None, "tp"),
        P("tp", None),
        P("tp", None),
        P("row", ("tp", "col")),
    )
    out_specs = (P("row", ("tp", "col")), P("row", "tp"))
    return jax.shard_map(
        per_device, mesh=mesh, in_specs=in_specs, out_specs=out_specs, check_vma=False
    )
```

time: 598 us -> 535 us (0.89)
  waiting for transfers between devices: 245 us -> 395 us
  other arithmetic: 135 us -> 12.4 us
  local copies, waits for them, and re-layouts: 59.6 us -> 11.2 us
  blocking collectives: 37.4 us -> 0 us
  Pallas kernels: 0 us -> 19.5 us
  matrix products: 87.9 us -> 78.2 us
  starting transfers between devices: 8.79 us -> 0.38 us
    another operation x18 -> x0, other arithmetic: 121 us -> none  [the longest x14 79 us: per_device(): diag_factor = jnp.linalg.cholesky(diag_block)]
    psum x2 -> x3, waiting for transfers between devices: 237 us -> 325 us  [the longest x1 127 us: per_device(): lax.psum(jnp.where(first_col & first_row, curvature[:panel_w, :panel_w],...]
    all_gather x0 -> x1, waiting for transfers between devices: none -> 47.8 us  [per_device(): feats = lax.all_gather(local, ('tp', 'row', 'col'), axis=0)]
    all_gather x2 -> x0, blocking collectives: 37.4 us -> none  [the longest x1 27.6 us: per_device(): lax.all_gather(quart_mine[None], ('tp', 'col'), axis=0, tiled=True)]
    unnamed x31 -> x14, local copies, waits for them, and re-layouts: 41 us -> 4.9 us
    another operation x20 -> x0, matrix products: 30.8 us -> none  [the longest x7 16 us: per_device(): jax.scipy.linalg.solve_triangular(diag_factor, top_block, lower=True)]
    dot_general x2 -> x8, matrix products: 47.1 us -> 71.4 us  [the longest x4 31.1 us: gram(): lax.dot_general(a, b, (((0,), (0,)), ((), ())), preferred_element_type=jn...]
    pallas_call x0 -> x1, Pallas kernels: none -> 19.5 us  [factor_inverse(): pl.pallas_call(inverse_kernel, out_shape=jax.ShapeDtypeStruct((n, n), jnp...]
  transfers between devices with their start and end apart: 5 -> 5, of which waited for: 4 -> 5; matrix products, arithmetic and copies ran while one was open for 4% -> 6% of each run, Pallas kernels for 0% -> 4%
where the time goes in v1:
time: 535 us; the launch traced here: 531 us
  waiting for transfers between devices  395 us (74%)
  matrix products  78.2 us (15%)
  Pallas kernels  19.5 us (4%)
  between operations  14.4 us (3%)
  other arithmetic  12.4 us (2%)
  local copies, waits for them, and re-layouts  11.2 us (2%)
    psum x1, waiting for transfers between devices, per_device(): lax.psum(jnp.where(first_col & first_row, curvature[:panel_w, :panel_w],...  127 us
    psum x1, waiting for transfers between devices, per_device(): lax.psum(jnp.where(first_col, curvature[:, :panel_w], zero), ('tp', 'col'))  110 us
    psum x1, waiting for transfers between devices, per_device(): top_raw = lax.psum(jnp.where(first_row, curvature[:panel_w], zero), 'row')  88 us
    all_gather x1, waiting for transfers between devices, per_device(): feats = lax.all_gather(local, ('tp', 'row', 'col'), axis=0)  47.8 us
    dot_general x4, matrix products, gram(): lax.dot_general(a, b, (((0,), (0,)), ((), ())), preferred_element_type=jn...  31.1 us
    psum x1, waiting for transfers between devices, per_device(): proj_acts, proj_grads = lax.psum((act_part, grad_part), 'tp')  22.5 us
    pallas_call x1, Pallas kernels, factor_inverse(): pl.pallas_call(inverse_kernel, out_shape=jax.ShapeDtypeStruct((n, n), jnp...  19.5 us
    dot_general x1, matrix products, per_device(): jnp.dot(panel_rows, top_factor, precision=lax.Precision.HIGH, preferred_e...  18.4 us
  transfers between devices with their start and end apart: 5, of which 5 were waited for; matrix products, arithmetic and copies ran while one was open for 6% of the time, Pallas kernels for 4%

profile of v1, /device:TPU:0, one launch (start us, length us, event | category | flops | bytes accessed | tf_op | source)
XLA Modules:
  0.0 531.3 jit_solution(4550895367845079587)
XLA Ops:
  7.2 0.0 all-reduce.12.cloned.1.call-start
  7.2 1.1 copy-done
  8.3 4.7 fusion.6
  13.1 2.1 fusion.15
  15.2 0.0 all-reduce.12.cloned.1.call-update
  15.2 0.0 all-gather.2.cloned.1.call-start
  15.3 22.5 %all-reduce.12.cloned.1.call-done = (f32[8,128,64]{1,2,0:T(8,128)}, f32[8,128,192]{1,2,0:T(8,128)}) async-done(((f32[8,128,64]{1,2,0:T(8,128)}, f32[8,128,192]{1,2,0:T(8,128)}), (f32[8,128,64]{1,2,0:T(8,128)}, f32[8,128,192]{1,2,0:T(8,128)})) %all-reduce.12.cloned.1.call-update) | async-done | bytes 1048592 | tf_op jit(solution)/shard_map/psum | solution.py:133
  37.7 1.9 fusion.2
  39.6 0.2 copy.8
  39.8 0.9 all_gather_reshape.3
  40.7 0.0 all-reduce.8.cloned.1.call-start
  40.7 2.3 slice_select_fusion.2
  43.1 0.0 all-reduce.10.cloned.1.call-start
  43.1 3.8 slice_select_fusion.1
  46.9 0.2 all-reduce.6.cloned.1.call-start
  47.2 6.3 %slice_select_fusion = f32[3072,512]{1,0:T(8,128)} fusion(f32[3072,1536]{1,0:T(8,128)} %param.9, pred[]{:T(512)S(6)} %eq.9), kind=kLoop, calls=%fused_computation.3 | loop fusion | flops 1572864 | bytes 12582913 | tf_op jit(solution)/shard_map/jit(_where)/select_n | solution.py:123
  53.5 47.8 %all-gather.2.cloned.1.call-done = bf16[32,8,6144]{2,1,0:T(8,128)(2,1)} async-done(((bf16[1,8,6144]{2,1,0:T(8,128)(2,1)}), bf16[32,8,6144]{2,1,0:T(8,128)(2,1)}) %all-gather.2.cloned.1.call-update) | async-done | bytes 3145744 | tf_op jit(solution)/shard_map/all_gather | solution.py:140
  101.3 1.5 slice_bitcast_fusion
  102.8 1.2 copy-done.5
  104.0 4.9 fusion.3
  108.9 127.1 %all-reduce.8.cloned.1.call-done = f32[512,512]{1,0:T(8,128)} async-done(((f32[512,512]{1,0:T(8,128)}), f32[512,512]{1,0:T(8,128)}) %all-reduce.8.cloned.1.call-update) | async-done | bytes 1048592 | tf_op jit(solution)/shard_map/psum | solution.py:118
  235.9 1.7 convolution_add_fusion.1.a_ref
  237.6 88.0 %all-reduce.10.cloned.1.call-done = f32[512,1536]{1,0:T(8,128)} async-done(((f32[512,1536]{1,0:T(8,128)}), f32[512,1536]{1,0:T(8,128)}) %all-reduce.10.cloned.1.call-update) | async-done | bytes 3145744 | tf_op jit(solution)/shard_map/psum | solution.py:125
  325.6 2.7 convolution_add_fusion
  328.4 19.5 %shard_map.68 = f32[512,512]{1,0:T(8,128)S(1)} custom-call(f32[512,512]{1,0:T(8,128)S(1)} %convolution_add_fusion.1.a_ref), custom_call_target="tpu_custom_call" | custom-call | flops 40000000000 | bytes 2097152 | tf_op jit(solution)/shard_map/pallas_call | solution.py:86
  348.0 6.9 %fusion.24 = f32[512,1536]{1,0:T(8,128)} fusion(f32[512,512]{1,0:T(8,128)S(1)} %shard_map.68, f32[512,1536]{1,0:T(8,128)S(1)} %convolution_add_fusion), kind=kOutput, calls=%fused_computation.33 | convolution fusion | flops 4831838208 | bytes 7340032 | tf_op jit(solution)/shard_map/dot_general | solution.py:172
  354.8 109.8 %all-reduce.6.cloned.1.call-done = f32[3072,512]{1,0:T(8,128)} async-done(((f32[3072,512]{1,0:T(8,128)}), f32[3072,512]{1,0:T(8,128)}) %all-reduce.6.cloned.1.call-update) | async-done | bytes 6291472 | tf_op jit(solution)/shard_map/psum | solution.py:122
  464.7 13.1 %fusion = f32[3072,512]{1,0:T(8,128)S(1)} fusion(f32[512,512]{1,0:T(8,128)S(1)} %shard_map.68, f32[3072,512]{1,0:T(8,128)} %all-reduce.6.cloned.1.call-done, f32[3072,512]{1,0:T(8,128)} %fusion.3), kind=kOutput, calls=%fused_computation.1 | convolution fusion | flops 9665249280 | bytes 19922944 | tf_op jit(solution)/shard_map/dot_general | solution.py:165
  477.7 2.6 copy-done.2
  480.4 18.4 %fusion.25 = f32[3072,1536]{1,0:T(8,128)} fusion(f32[3072,512]{1,0:T(8,128)S(1)} %fusion, f32[512,1536]{1,0:T(8,128)S(1)} %copy-done.3), kind=kOutput, calls=%fused_computation.34 | convolution fusion | flops 14495514624 | bytes 28311552 | tf_op jit(solution)/shard_map/dot_general | solution.py:175
  498.8 21.8 %add_subtract_fusion = f32[3072,1536]{1,0:T(8,128)} fusion(f32[3072,1536]{1,0:T(8,128)} %fusion.25, f32[3072,1536]{1,0:T(8,128)} %param.9, bf16[2,128,6144]{2,1,0:T(8,128)(2,1)} %bitcast.29, s32[]{:T(128)S(6)} %select_n.62, s32[]{:T(128)S(6)} %select_n.64, s32[]{:T(128)S(6)} %select_n.66, s32[]{:T(128)S(6)} %select_n.68), kind=kOutput, calls=%fused_computation | convolution fusion | flops 1217396736 | bytes 57802768 | tf_op jit(solution)/shard_map/dot_general | solution.py:158
  520.6 3.8 constant_dynamic-slice_fusion
  (15 shorter events, 0.1 us)
Async XLA Ops:
  7.2 1.1 copy-start
  7.2 5.9 %copy-start.6 = (bf16[2048,64]{0,1:T(8,128)(2,1)S(1)}, bf16[2048,64]{0,1:T(8,128)(2,1)}, u32[]{:S(2)}) copy-start(bf16[2048,64]{0,1:T(8,128)(2,1)} %param.8) | copy-start | bytes 786436
  7.2 30.5 %all-reduce.12.cloned.1.call-start = ((), (), s32[]{:S(2)}) async-start(), calls=%async_computation.4 | async-start | bytes 2097152 | tf_op jit(solution)/shard_map/psum | solution.py:133
  8.3 4.8 copy-start.4
  15.2 86.1 %all-gather.2.cloned.1.call-start = ((), (), s32[]{:S(2)}) async-start(), calls=%async_computation | async-start | bytes 3244032 | tf_op jit(solution)/shard_map/all_gather | solution.py:140
  40.7 195.3 %all-reduce.8.cloned.1.call-start = ((), (), s32[]{:S(2)}) async-start(), calls=%async_computation.2 | async-start | bytes 2097152 | tf_op jit(solution)/shard_map/psum | solution.py:118
  43.1 282.6 %all-reduce.10.cloned.1.call-start = ((), (), s32[]{:S(2)}) async-start(), calls=%async_computation.3 | async-start | bytes 6291456 | tf_op jit(solution)/shard_map/psum | solution.py:125
  46.9 417.7 %all-reduce.6.cloned.1.call-start = ((), (), s32[]{:S(2)}) async-start(), calls=%async_computation.1 | async-start | bytes 12582912 | tf_op jit(solution)/shard_map/psum | solution.py:122
  102.8 1.2 copy-start.5
  464.7 15.7 %copy-start.3 = (f32[512,1536]{1,0:T(8,128)S(1)}, f32[512,1536]{1,0:T(8,128)}, u32[]{:S(2)}) copy-start(f32[512,1536]{1,0:T(8,128)} %fusion.24) | copy-start | bytes 9437188
  477.7 2.7 copy-start.2
  498.8 25.6 %copy-start.1 = (bf16[2048,192]{0,1:T(8,128)(2,1)S(1)}, bf16[2048,192]{0,1:T(8,128)(2,1)}, u32[]{:S(2)}) copy-start(bf16[2048,192]{0,1:T(8,128)(2,1)} %param.7) | copy-start | bytes 2359300
Sparse Core Ops, SparseCore 0:
  15.3 22.3 all-reduce.11
  41.0 60.2 all-gather.1
  107.3 128.5 all-reduce.7
  239.4 86.1 all-reduce.9
  328.6 136.0 all-reduce.5
